TPU v7x, 512 devices: a whole 4x4x16 slice. The times are simulated.
512 devices in a mesh: modes: 16 (over y, x_lo, core), sites: 32 (over x_hi, z).
Axes of the slice: x: 4 (x_hi: 2, x_lo: 2; x = x_hi * 2 + x_lo), y: 4, z: 16, core: 2. Of those that a mesh axis runs over, the one named last changes fastest.
Arguments:
- wave_state: float32 [4, 128, 131072], P(None, 'modes', 'sites'), may hold values from -6 to 6
- potential: float32 [131072], P('sites'), may hold values from -0.5 to 0.5
- spin_angle: float32 [131072], P('sites'), may hold values from -3.140625 to 3.140625
- magnet: float32 [3, 131072], P(None, 'sites'), may hold values from -0.6 to 0.6
- magnetic_mask: int32 [131072], P('sites'), may hold values 0 or 1
- mode_weight: float32 [128], P('modes'), may hold values from 0.5 to 2
- source_amp: float32 [4, 128], P(None, 'modes'), may hold values from -6 to 6
- mode_group: int32 [128], P('modes'), may hold values from 0 to 7
- energies: float32 [8], replicated, may hold values from -2 to 2
- lead_site: int32 [128], P('modes'), may hold values from 0 to 131071
Outputs:
- next_state: float32 [4, 128, 131072], P(None, 'modes', 'sites')
- densities: float32 [5, 131072], P(None, 'sites')
- magnet_next: float32 [3, 131072], P(None, 'sites')
All inputs are finite; a program needn't handle non-finite values. No bound on the sum of `magnetic_mask` on one device may be relied on, other than what follows from the above.
Results may differ from a plain program's by a relative error of at most 0.0001.
Values sent between devices are 32-bit elements; how exact they have to be, the bound alone decides.
A program may use at most 64 MiB of HBM per device.

v0:
```python
import math
import jax
import jax.numpy as jnp
from jax import lax
from jax.sharding import PartitionSpec as P

time_step = 0.6
start_time = 10.0
exchange_coupling = 0.5


def extended(cells, sides, width):
    for axis, dim in sides:
        count = lax.axis_size(axis)
        ends = count - 1
        head = lax.slice_in_dim(cells, 0, width, axis=dim)
        tail = lax.slice_in_dim(cells, cells.shape[dim] - width, cells.shape[dim], axis=dim)
        cells = jnp.concatenate(
            [
                lax.ppermute(tail, axis, [(i, (i + 1) % count) for i in range(ends)]),
                cells,
                lax.ppermute(head, axis, [((i + 1) % count, i) for i in range(ends)]),
            ],
            axis=dim,
        )
    return cells


def rotate_back(spinor, cosine, sine_term):
    shaped = spinor.reshape((2, 2) + spinor.shape[1:])
    spin_up = shaped[:, 0]
    spin_down = shaped[:, 1]
    turned = jnp.stack(
        [cosine * spin_up + sine_term * spin_down, cosine * spin_down - sine_term * spin_up], axis=1
    )
    return turned.reshape(spinor.shape)


def rotate_fore(spinor, cosine, sine_term):
    shaped = spinor.reshape((2, 2) + spinor.shape[1:])
    spin_up = shaped[:, 0]
    spin_down = shaped[:, 1]
    turned = jnp.stack(
        [cosine * spin_up - sine_term * spin_down, sine_term * spin_up + cosine * spin_down], axis=1
    )
    return turned.reshape(spinor.shape)


def exchange_term(spinor, sd_field):
    up_real, down_real, up_imag, down_imag = (spinor[0], spinor[1], spinor[2], spinor[3])
    field_x, field_y, field_z = (sd_field[0], sd_field[1], sd_field[2])
    out_up_real = field_z * up_real + field_x * down_real + field_y * down_imag
    out_down_real = field_x * up_real - field_y * up_imag - field_z * down_real
    out_up_imag = field_z * up_imag + field_x * down_imag - field_y * down_real
    out_down_imag = field_x * up_imag + field_y * up_real - field_z * down_imag
    return jnp.stack([out_up_real, out_down_real, out_up_imag, out_down_imag])


def source_field(offset, amplitude, energy, region):
    phase_angle = energy * (start_time + offset)
    cosine_phase = jnp.cos(phase_angle)
    sine_phase = jnp.sin(phase_angle)
    amp_real = amplitude[0:2]
    amp_imag = amplitude[2:4]
    real_part = amp_real * cosine_phase + amp_imag * sine_phase
    imag_part = amp_imag * cosine_phase - amp_real * sine_phase
    joined = jnp.concatenate([real_part, imag_part], axis=0)
    return joined[:, :, None] * region[None]


def rate(spinor, left_w, right_w, cosine, sine_term, potential, sd_field, source):
    hamil_term = (
        potential * spinor
        + exchange_term(spinor, sd_field)
        - rotate_fore(left_w + right_w, cosine, sine_term)
        + source
    )
    return jnp.concatenate([hamil_term[2:], -hamil_term[:2]], axis=0)


def densities_of(spinor, right_w, cosine, sine_term, weight_vec):
    up_real, down_real, up_imag, down_imag = (spinor[0], spinor[1], spinor[2], spinor[3])
    hopped = rotate_fore(right_w, cosine, sine_term)
    charge = up_real * up_real + down_real * down_real + up_imag * up_imag + down_imag * down_imag
    spin_x = 2.0 * (up_real * down_real + up_imag * down_imag)
    spin_y = 2.0 * (up_real * down_imag - up_imag * down_real)
    spin_z = up_real * up_real + up_imag * up_imag - down_real * down_real - down_imag * down_imag
    current = 2.0 * (
        up_real * hopped[2] + down_real * hopped[3] - up_imag * hopped[0] - down_imag * hopped[1]
    )
    stacked = jnp.stack([charge, spin_x, spin_y, spin_z, current])
    return jnp.sum(stacked * weight_vec[None, :, None], axis=1)


def advance(magnet, mask_float, totals):
    field_h = exchange_coupling * totals[1:4]
    torque = jnp.stack(
        [
            magnet[1] * field_h[2] - magnet[2] * field_h[1],
            magnet[2] * field_h[0] - magnet[0] * field_h[2],
            magnet[0] * field_h[1] - magnet[1] * field_h[0],
        ]
    )
    return magnet - time_step * (mask_float * torque)


def source_region(positions, lead_site, region_span):
    return (
        (positions[None, :] >= lead_site[:, None])
        & (positions[None, :] < lead_site[:, None] + region_span)
    ).astype(jnp.float32)


def local(
    wave_state,
    potential,
    spin_angle,
    magnet,
    magnetic_mask,
    mode_weight,
    source_amp,
    mode_group,
    energies,
    lead_site,
):
    local_sites = wave_state.shape[2]
    local_modes = wave_state.shape[1]
    site_count = lax.axis_size("sites")
    mode_count = lax.axis_size("modes")
    first_site = lax.axis_index("sites") * local_sites
    wire_sites = local_sites * site_count
    region_span = wire_sites // 8
    all_modes = local_modes * mode_count
    mask_float = magnetic_mask.astype(jnp.float32)
    group_ids = jnp.arange(energies.shape[0], dtype=jnp.int32)
    mode_energy = jnp.sum(
        jnp.where(
            mode_group[:, None] == group_ids[None, :],
            energies[None, :],
            jnp.zeros_like(energies)[None, :],
        ),
        axis=1,
    )
    cosine = jnp.cos(spin_angle)
    sine_term = jnp.sin(spin_angle)
    positions = first_site + jnp.arange(local_sites, dtype=jnp.int32)
    region = source_region(positions, lead_site, region_span)
    sd_field = exchange_coupling * mask_float * magnet

    def slope(spin_state, offset):
        weighted = rotate_back(spin_state, cosine, sine_term)
        padded = extended(weighted, (("sites", 2),), 1)
        source = source_field(offset, source_amp, mode_energy, region)
        return (
            rate(
                spin_state,
                padded[..., :-2],
                padded[..., 2:],
                cosine,
                sine_term,
                potential,
                sd_field,
                source,
            ),
            padded,
        )

    slope_one, padded_one = slope(wave_state, 0.0)
    slope_two, ignored = slope(wave_state + 0.5 * time_step * slope_one, 0.5 * time_step)
    slope_three, ignored = slope(wave_state + 0.5 * time_step * slope_two, 0.5 * time_step)
    slope_four, ignored = slope(wave_state + time_step * slope_three, time_step)
    next_state = wave_state + time_step / 6.0 * (
        slope_one + 2.0 * slope_two + 2.0 * slope_three + slope_four
    )
    right_w = padded_one[..., 2:]
    root_scale = 1.0 / math.sqrt(all_modes)
    row_scale = jnp.array(
        [1.0 / all_modes, root_scale, root_scale, root_scale, root_scale], jnp.float32
    )
    partial_value = (
        densities_of(wave_state, right_w, cosine, sine_term, mode_weight) * row_scale[:, None]
    )
    totals = lax.psum(partial_value, "modes")
    magnet_next = advance(magnet, mask_float, totals)
    return (next_state, totals, magnet_next)


def solution(mesh):
    return jax.shard_map(
        local,
        mesh=mesh,
        in_specs=(
            P(None, "modes", "sites"),
            P("sites"),
            P("sites"),
            P(None, "sites"),
            P("sites"),
            P("modes"),
            P(None, "modes"),
            P("modes"),
            P(),
            P("modes"),
        ),
        out_specs=(P(None, "modes", "sites"), P(None, "sites"), P(None, "sites")),
        check_vma=False,
    )
```

profile of v0, /device:TPU:1, one launch (start us, length us, event | category | flops | bytes accessed | tf_op | source)
XLA Modules:
  0.0 178.2 jit_solution(14860616858366607334)
XLA Ops:
  7.2 0.8 fusion.28
  8.0 1.1 multiply_add_fusion.13
  9.2 4.5 %collective-permute-start = (f32[4,8,1]{2,1,0:T(8,128)S(1)}, f32[4,8,1]{2,1,0:T(8,128)S(1)}, u32[]{:S(2)}, u32[]{:S(2)}) collective-permute-start(f32[4,8,1]{2,1,0:T(8,128)S(1)} %get-tuple-element.55), channel_id=1, source_target_pairs={{0,1},{1,2},{2,3},{3,4},{4,5},{5,6},{6,7},{7,8},{8,9},{9,10},{10,1... | collective-permute-start | bytes 392 | tf_op jit(solution)/shard_map/ppermute | solution.py:20
  13.7 1.3 collective-permute-start.1
  15.4 0.6 copy-done.13
  16.3 0.6 copy-done.10
  17.1 0.7 copy-done.9
  17.7 0.6 pad_maximum_fusion.20
  18.3 0.6 pad_maximum_fusion.22
  18.9 0.6 convert_element_type.10
  20.1 0.6 copy-done.3
  21.2 0.7 fusion.24
  21.9 4.8 %collective-permute-start.2 = (f32[4,8,1]{2,1,0:T(8,128)}, f32[4,8,1]{2,1,0:T(8,128)}, u32[]{:S(2)}, u32[]{:S(2)}) collective-permute-start(f32[4,8,1]{2,1,0:T(8,128)} %get-tuple-element.50), channel_id=1, source_target_pairs={{0,1},{1,2},{2,3},{3,4},{4,5},{5,6},{6,7},{7,8},{8,9},{9,10},{10,1... | collective-permute-start | bytes 392 | tf_op jit(solution)/shard_map/ppermute | solution.py:20
  26.6 1.3 collective-permute-start.3
  28.0 0.6 copy-done.12
  28.8 0.4 copy-done.11
  29.2 0.7 broadcast_multiply_fusion
  30.0 1.4 collective-permute-done.3
  31.4 1.1 fusion.2
  32.6 0.7 copy-done.4
  33.7 4.4 %collective-permute-start.4 = (f32[4,8,1]{2,1,0:T(8,128)S(1)}, f32[4,8,1]{2,1,0:T(8,128)S(1)}, u32[]{:S(2)}, u32[]{:S(2)}) collective-permute-start(f32[4,8,1]{2,1,0:T(8,128)S(1)} %get-tuple-element.46), channel_id=1, source_target_pairs={{0,1},{1,2},{2,3},{3,4},{4,5},{5,6},{6,7},{7,8},{8,9},{9,10},{10,1... | collective-permute-start | bytes 392 | tf_op jit(solution)/shard_map/ppermute | solution.py:20
  38.1 1.3 collective-permute-start.5
  39.5 4.3 %collective-permute-done.5 = f32[4,8,1]{2,1,0:T(8,128)S(1)} collective-permute-done((f32[4,8,1]{2,1,0:T(8,128)S(1)}, f32[4,8,1]{2,1,0:T(8,128)S(1)}, u32[]{:S(2)}, u32[]{:S(2)}) %collective-permute-start.5) | collective-permute-done | bytes 160 | tf_op jit(solution)/shard_map/ppermute | solution.py:22
  44.7 4.6 %collective-permute-start.6 = (f32[4,8,1]{2,1,0:T(8,128)S(1)}, f32[4,8,1]{2,1,0:T(8,128)S(1)}, u32[]{:S(2)}, u32[]{:S(2)}) collective-permute-start(f32[4,8,1]{2,1,0:T(8,128)S(1)} %get-tuple-element.42), channel_id=1, source_target_pairs={{0,1},{1,2},{2,3},{3,4},{4,5},{5,6},{6,7},{7,8},{8,9},{9,10},{10,1... | collective-permute-start | bytes 392 | tf_op jit(solution)/shard_map/ppermute | solution.py:20
  49.3 1.3 collective-permute-start.7
  50.7 3.1 %collective-permute-done.7 = f32[4,8,1]{2,1,0:T(8,128)S(1)} collective-permute-done((f32[4,8,1]{2,1,0:T(8,128)S(1)}, f32[4,8,1]{2,1,0:T(8,128)S(1)}, u32[]{:S(2)}, u32[]{:S(2)}) %collective-permute-start.7) | collective-permute-done | bytes 160 | tf_op jit(solution)/shard_map/ppermute | solution.py:22
  54.2 0.7 copy-done.8
  55.1 1.0 fusion.11
  56.1 112.7 %all-reduce.2.cloned.1.call-done = f32[5,4096]{1,0:T(8,128)} async-done(((f32[5,4096]{1,0:T(8,128)}), f32[5,4096]{1,0:T(8,128)}) %all-reduce.2.cloned.1.call-update) | async-done | bytes 81936 | tf_op jit(solution)/shard_map/psum | solution.py:183
  168.8 0.9 slice_multiply_fusion.4
  169.8 0.7 fusion.18
  170.7 0.7 copy.19
  (80 shorter events, 4.6 us)
Async XLA Ops:
  7.2 161.7 %all-reduce.2.cloned.1.call-start = ((), (), s32[]{:S(2)}) async-start(), calls=%async_computation | async-start | bytes 262144 | tf_op jit(solution)/shard_map/psum | solution.py:183
  9.1 6.0 %copy-start.6 = (s32[4096]{0:T(1024)S(1)}, s32[4096]{0:T(1024)}, u32[]{:S(2)}) copy-start(s32[4096]{0:T(1024)} %param.15) | copy-start | bytes 49156
  9.1 6.1 %copy-start = (f32[4,8,4096]{2,1,0:T(8,128)S(1)}, f32[4,8,4096]{2,1,0:T(8,128)}, u32[]{:S(2)}) copy-start(f32[4,8,4096]{2,1,0:T(8,128)} %param.11) | copy-start | bytes 1572868
  9.2 5.9 %copy-start.1 = (f32[3,4096]{1,0:T(4,128)S(1)}, f32[3,4096]{1,0:T(4,128)}, u32[]{:S(2)}) copy-start(f32[3,4096]{1,0:T(4,128)} %param.14) | copy-start | bytes 147460
  9.2 10.3 %collective-permute-start = (f32[4,8,1]{2,1,0:T(8,128)S(1)}, f32[4,8,1]{2,1,0:T(8,128)S(1)}, u32[]{:S(2)}, u32[]{:S(2)}) collective-permute-start(f32[4,8,1]{2,1,0:T(8,128)S(1)} %get-tuple-element.55), channel_id=1, source_target_pairs={{0,1},{1,2},{2,3},{3,4},{4,5},{5,6},{6,7},{7,8},{8,9},{9,10},{10,1... | collective-permute-start | bytes 392 | tf_op jit(solution)/shard_map/ppermute | solution.py:20
  13.7 5.8 %collective-permute-start.1 = (f32[4,8,1]{2,1,0:T(8,128)S(1)}, f32[4,8,1]{2,1,0:T(8,128)S(1)}, u32[]{:S(2)}, u32[]{:S(2)}) collective-permute-start(f32[4,8,1]{2,1,0:T(8,128)S(1)} %get-tuple-element.54), channel_id=1, source_target_pairs={{1,0},{2,1},{3,2},{4,3},{5,4},{6,5},{7,6},{8,7},{9,8},{10,9},{11,1... | collective-permute-start | bytes 392 | tf_op jit(solution)/shard_map/ppermute | solution.py:22
  15.4 0.7 copy-start.13
  15.4 0.7 copy-start.14
  16.3 0.7 copy-start.10
  17.1 0.7 copy-start.9
  20.0 0.7 copy-start.3
  21.9 8.1 %collective-permute-start.2 = (f32[4,8,1]{2,1,0:T(8,128)}, f32[4,8,1]{2,1,0:T(8,128)}, u32[]{:S(2)}, u32[]{:S(2)}) collective-permute-start(f32[4,8,1]{2,1,0:T(8,128)} %get-tuple-element.50), channel_id=1, source_target_pairs={{0,1},{1,2},{2,3},{3,4},{4,5},{5,6},{6,7},{7,8},{8,9},{9,10},{10,1... | collective-permute-start | bytes 392 | tf_op jit(solution)/shard_map/ppermute | solution.py:20
  26.6 4.8 %collective-permute-start.3 = (f32[4,8,1]{2,1,0:T(8,128)}, f32[4,8,1]{2,1,0:T(8,128)}, u32[]{:S(2)}, u32[]{:S(2)}) collective-permute-start(f32[4,8,1]{2,1,0:T(8,128)} %get-tuple-element.51), channel_id=1, source_target_pairs={{1,0},{2,1},{3,2},{4,3},{5,4},{6,5},{7,6},{8,7},{9,8},{10,9},{11,1... | collective-permute-start | bytes 392 | tf_op jit(solution)/shard_map/ppermute | solution.py:22
  27.9 0.7 copy-start.12
  28.6 0.7 copy-start.11
  32.6 0.7 copy-start.4
  32.6 0.7 copy-start.7
  33.7 5.8 %collective-permute-start.4 = (f32[4,8,1]{2,1,0:T(8,128)S(1)}, f32[4,8,1]{2,1,0:T(8,128)S(1)}, u32[]{:S(2)}, u32[]{:S(2)}) collective-permute-start(f32[4,8,1]{2,1,0:T(8,128)S(1)} %get-tuple-element.46), channel_id=1, source_target_pairs={{0,1},{1,2},{2,3},{3,4},{4,5},{5,6},{6,7},{7,8},{8,9},{9,10},{10,1... | collective-permute-start | bytes 392 | tf_op jit(solution)/shard_map/ppermute | solution.py:20
  38.1 5.7 %collective-permute-start.5 = (f32[4,8,1]{2,1,0:T(8,128)S(1)}, f32[4,8,1]{2,1,0:T(8,128)S(1)}, u32[]{:S(2)}, u32[]{:S(2)}) collective-permute-start(f32[4,8,1]{2,1,0:T(8,128)S(1)} %get-tuple-element.47), channel_id=1, source_target_pairs={{1,0},{2,1},{3,2},{4,3},{5,4},{6,5},{7,6},{8,7},{9,8},{10,9},{11,1... | collective-permute-start | bytes 392 | tf_op jit(solution)/shard_map/ppermute | solution.py:22
  44.7 6.0 %collective-permute-start.6 = (f32[4,8,1]{2,1,0:T(8,128)S(1)}, f32[4,8,1]{2,1,0:T(8,128)S(1)}, u32[]{:S(2)}, u32[]{:S(2)}) collective-permute-start(f32[4,8,1]{2,1,0:T(8,128)S(1)} %get-tuple-element.42), channel_id=1, source_target_pairs={{0,1},{1,2},{2,3},{3,4},{4,5},{5,6},{6,7},{7,8},{8,9},{9,10},{10,1... | collective-permute-start | bytes 392 | tf_op jit(solution)/shard_map/ppermute | solution.py:20
  49.3 4.5 %collective-permute-start.7 = (f32[4,8,1]{2,1,0:T(8,128)S(1)}, f32[4,8,1]{2,1,0:T(8,128)S(1)}, u32[]{:S(2)}, u32[]{:S(2)}) collective-permute-start(f32[4,8,1]{2,1,0:T(8,128)S(1)} %get-tuple-element.43), channel_id=1, source_target_pairs={{1,0},{2,1},{3,2},{4,3},{5,4},{6,5},{7,6},{8,7},{9,8},{10,9},{11,1... | collective-permute-start | bytes 392 | tf_op jit(solution)/shard_map/ppermute | solution.py:22
  54.2 0.7 copy-start.8
  55.1 114.8 %copy-start.5 = (f32[4096]{0:T(1024)S(1)}, f32[4096]{0:T(1024)}, u32[]{:S(2)}) copy-start(f32[4096]{0:T(1024)} %convert_element_type.10) | copy-start | bytes 49156
  169.8 0.9 copy-start.2
Sparse Core Ops, SparseCore 0:
  30.1 138.6 all-reduce.1
where the time goes:
time: 179 us; the launch traced here: 178 us
  waiting for transfers between devices  122 us (68%)
  starting transfers between devices  23.4 us (13%)
  between operations  14.6 us (8%)
  other arithmetic  11.3 us (6%)
  local copies, waits for them, and re-layouts  7.48 us (4%)
    psum x1, waiting for transfers between devices, local(): totals = lax.psum(partial_value, 'modes')  113 us
    ppermute x4, starting transfers between devices, extended(): lax.ppermute(tail, axis, [(i, (i + 1) % count) for i in range(ends)])  18.2 us
    ppermute x4, waiting for transfers between devices, extended(): lax.ppermute(head, axis, [((i + 1) % count, i) for i in range(ends)])  8.79 us
    unnamed x31, local copies, waits for them, and re-layouts  5.75 us
    ppermute x4, starting transfers between devices, extended(): lax.ppermute(head, axis, [((i + 1) % count, i) for i in range(ends)])  5.16 us
  transfers between devices with their start and end apart: 9, of which 4 were waited for; matrix products, arithmetic and copies ran while one was open for 4% of the time, Pallas kernels for 0%

commit v1 on v0

--- a/solution.py
+++ b/solution.py
@@ -180,7 +180,8 @@
     partial_value = (
         densities_of(wave_state, right_w, cosine, sine_term, mode_weight) * row_scale[:, None]
     )
-    totals = lax.psum(partial_value, "modes")
+    parts = lax.all_gather(partial_value, "modes")
+    totals = jnp.sum(parts, axis=0)
     magnet_next = advance(magnet, mask_float, totals)
     return (next_state, totals, magnet_next)
 

time: 179 us -> 86.9 us (0.49)
  waiting for transfers between devices: 122 us -> 34.3 us
  local copies, waits for them, and re-layouts: 7.48 us -> 2.37 us
    psum x1 -> x0, waiting for transfers between devices: 113 us -> none  [local(): totals = lax.psum(partial_value, 'modes')]
    all_gather x0 -> x1, waiting for transfers between devices: none -> 24.1 us  [local(): parts = lax.all_gather(partial_value, 'modes')]
    unnamed x31 -> x30, local copies, waits for them, and re-layouts: 5.75 us -> 0.59 us
  transfers between devices with their start and end apart: 9 -> 9, of which waited for: 4 -> 5; matrix products, arithmetic and copies ran while one was open for 4% -> 9% of each run, Pallas kernels for 0% -> 0%
where the time goes in v1:
time: 86.9 us; the launch traced here: 86.3 us
  waiting for transfers between devices  34.3 us (39%)
  starting transfers between devices  22.8 us (26%)
  between operations  14.7 us (17%)
  other arithmetic  12.1 us (14%)
  local copies, waits for them, and re-layouts  2.37 us (3%)
    all_gather x1, waiting for transfers between devices, local(): parts = lax.all_gather(partial_value, 'modes')  24.1 us
    ppermute x4, starting transfers between devices, extended(): lax.ppermute(tail, axis, [(i, (i + 1) % count) for i in range(ends)])  17.6 us
    ppermute x4, waiting for transfers between devices, extended(): lax.ppermute(head, axis, [((i + 1) % count, i) for i in range(ends)])  10.2 us
    ppermute x4, starting transfers between devices, extended(): lax.ppermute(head, axis, [((i + 1) % count, i) for i in range(ends)])  5.16 us
    add x3, other arithmetic, rate(): left_w + right_w  1.75 us
    reduce_sum x1, other arithmetic, local(): totals = jnp.sum(parts, axis=0)  1.74 us
  transfers between devices with their start and end apart: 9, of which 5 were waited for; matrix products, arithmetic and copies ran while one was open for 9% of the time, Pallas kernels for 0%

profile of v1, /device:TPU:1, one launch (start us, length us, event | category | flops | bytes accessed | tf_op | source)
XLA Modules:
  0.0 86.3 jit_solution(18144337857274606931)
XLA Ops:
  7.2 0.8 fusion.28
  8.1 1.1 %multiply_add_fusion.13 = (f32[2,1,8,4096]{3,2,1,0:T(8,128)S(1)}, f32[2,1,8,4096]{3,2,1,0:T(8,128)S(1)}) fusion(f32[2,2,8,4096]{3,2,1,0:T(8,128)} %bitcast.27, f32[4096]{0:T(1024)S(1)} %get-tuple-element.65, f32[4096]{0:T(1024)S(1)} %get-tuple-element.64), kind=kLoop, calls=%fused_computation.64 | loop fusion | flops 393216 | bytes 1081344 | tf_op jit(solution)/shard_map/add | solution.py:34
  9.3 4.4 %collective-permute-start = (f32[4,8,1]{2,1,0:T(8,128)S(1)}, f32[4,8,1]{2,1,0:T(8,128)S(1)}, u32[]{:S(2)}, u32[]{:S(2)}) collective-permute-start(f32[4,8,1]{2,1,0:T(8,128)S(1)} %get-tuple-element.55), channel_id=1, source_target_pairs={{0,1},{1,2},{2,3},{3,4},{4,5},{5,6},{6,7},{7,8},{8,9},{9,10},{10,1... | collective-permute-start | bytes 392 | tf_op jit(solution)/shard_map/ppermute | solution.py:20
  13.7 1.3 %collective-permute-start.1 = (f32[4,8,1]{2,1,0:T(8,128)S(1)}, f32[4,8,1]{2,1,0:T(8,128)S(1)}, u32[]{:S(2)}, u32[]{:S(2)}) collective-permute-start(f32[4,8,1]{2,1,0:T(8,128)S(1)} %get-tuple-element.54), channel_id=1, source_target_pairs={{1,0},{2,1},{3,2},{4,3},{5,4},{6,5},{7,6},{8,7},{9,8},{10,9},{11,1... | collective-permute-start | bytes 392 | tf_op jit(solution)/shard_map/ppermute | solution.py:22
  15.4 0.2 select_reduce_fusion
  15.8 0.6 pad_maximum_fusion.20
  16.4 0.6 pad_maximum_fusion.22
  17.0 0.6 convert_element_type.10
  17.6 0.8 collective-permute-done.1
  18.4 0.3 pad_maximum_fusion.6
  18.9 0.5 copy-done.3
  19.9 0.7 fusion.24
  20.6 4.1 %collective-permute-start.2 = (f32[4,8,1]{2,1,0:T(8,128)}, f32[4,8,1]{2,1,0:T(8,128)}, u32[]{:S(2)}, u32[]{:S(2)}) collective-permute-start(f32[4,8,1]{2,1,0:T(8,128)} %get-tuple-element.50), channel_id=1, source_target_pairs={{0,1},{1,2},{2,3},{3,4},{4,5},{5,6},{6,7},{7,8},{8,9},{9,10},{10,1... | collective-permute-start | bytes 392 | tf_op jit(solution)/shard_map/ppermute | solution.py:20
  24.7 1.3 %collective-permute-start.3 = (f32[4,8,1]{2,1,0:T(8,128)}, f32[4,8,1]{2,1,0:T(8,128)}, u32[]{:S(2)}, u32[]{:S(2)}) collective-permute-start(f32[4,8,1]{2,1,0:T(8,128)} %get-tuple-element.51), channel_id=1, source_target_pairs={{1,0},{2,1},{3,2},{4,3},{5,4},{6,5},{7,6},{8,7},{9,8},{10,9},{11,1... | collective-permute-start | bytes 392 | tf_op jit(solution)/shard_map/ppermute | solution.py:22
  26.1 0.3 multiply_reduce_fusion
  26.4 0.7 bitcast_multiply_fusion
  27.2 3.2 %collective-permute-done.3 = f32[4,8,1]{2,1,0:T(8,128)} collective-permute-done((f32[4,8,1]{2,1,0:T(8,128)}, f32[4,8,1]{2,1,0:T(8,128)}, u32[]{:S(2)}, u32[]{:S(2)}) %collective-permute-start.3) | collective-permute-done | bytes 160 | tf_op jit(solution)/shard_map/ppermute | solution.py:22
  30.4 1.1 %fusion.2 = f32[4,8,4096]{2,1,0:T(8,128)S(1)} fusion(f32[4,8,1]{2,1,0:T(8,128)} %collective-permute-done.3, f32[4,8,4096]{2,1,0:T(8,128)S(1)} %bitcast.34, f32[4,8,1]{2,1,0:T(8,128)} %collective-permute-done.2), kind=kLoop, calls=%fused_computation.10 | loop fusion | flops 393216 | bytes 1048832 | tf_op jit(solution)/shard_map/add | solution.py:75
  31.6 0.1 multiply_add_fusion.1
  32.0 4.6 %collective-permute-start.4 = (f32[4,8,1]{2,1,0:T(8,128)S(1)}, f32[4,8,1]{2,1,0:T(8,128)S(1)}, u32[]{:S(2)}, u32[]{:S(2)}) collective-permute-start(f32[4,8,1]{2,1,0:T(8,128)S(1)} %get-tuple-element.46), channel_id=1, source_target_pairs={{0,1},{1,2},{2,3},{3,4},{4,5},{5,6},{6,7},{7,8},{8,9},{9,10},{10,1... | collective-permute-start | bytes 392 | tf_op jit(solution)/shard_map/ppermute | solution.py:20
  36.6 1.3 %collective-permute-start.5 = (f32[4,8,1]{2,1,0:T(8,128)S(1)}, f32[4,8,1]{2,1,0:T(8,128)S(1)}, u32[]{:S(2)}, u32[]{:S(2)}) collective-permute-start(f32[4,8,1]{2,1,0:T(8,128)S(1)} %get-tuple-element.47), channel_id=1, source_target_pairs={{1,0},{2,1},{3,2},{4,3},{5,4},{6,5},{7,6},{8,7},{9,8},{10,9},{11,1... | collective-permute-start | bytes 392 | tf_op jit(solution)/shard_map/ppermute | solution.py:22
  38.0 3.1 %collective-permute-done.5 = f32[4,8,1]{2,1,0:T(8,128)S(1)} collective-permute-done((f32[4,8,1]{2,1,0:T(8,128)S(1)}, f32[4,8,1]{2,1,0:T(8,128)S(1)}, u32[]{:S(2)}, u32[]{:S(2)}) %collective-permute-start.5) | collective-permute-done | bytes 160 | tf_op jit(solution)/shard_map/ppermute | solution.py:22
  41.1 0.3 fusion.1
  41.6 0.1 multiply_add_fusion
  42.0 4.6 %collective-permute-start.6 = (f32[4,8,1]{2,1,0:T(8,128)S(1)}, f32[4,8,1]{2,1,0:T(8,128)S(1)}, u32[]{:S(2)}, u32[]{:S(2)}) collective-permute-start(f32[4,8,1]{2,1,0:T(8,128)S(1)} %get-tuple-element.42), channel_id=1, source_target_pairs={{0,1},{1,2},{2,3},{3,4},{4,5},{5,6},{6,7},{7,8},{8,9},{9,10},{10,1... | collective-permute-start | bytes 392 | tf_op jit(solution)/shard_map/ppermute | solution.py:20
  46.6 1.3 %collective-permute-start.7 = (f32[4,8,1]{2,1,0:T(8,128)S(1)}, f32[4,8,1]{2,1,0:T(8,128)S(1)}, u32[]{:S(2)}, u32[]{:S(2)}) collective-permute-start(f32[4,8,1]{2,1,0:T(8,128)S(1)} %get-tuple-element.43), channel_id=1, source_target_pairs={{1,0},{2,1},{3,2},{4,3},{5,4},{6,5},{7,6},{8,7},{9,8},{10,9},{11,1... | collective-permute-start | bytes 392 | tf_op jit(solution)/shard_map/ppermute | solution.py:22
  48.0 3.1 %collective-permute-done.7 = f32[4,8,1]{2,1,0:T(8,128)S(1)} collective-permute-done((f32[4,8,1]{2,1,0:T(8,128)S(1)}, f32[4,8,1]{2,1,0:T(8,128)S(1)}, u32[]{:S(2)}, u32[]{:S(2)}) %collective-permute-start.7) | collective-permute-done | bytes 160 | tf_op jit(solution)/shard_map/ppermute | solution.py:22
  51.1 0.3 fusion
  51.8 1.0 %fusion.11 = f32[4,8,4096]{2,1,0:T(8,128)} fusion(f32[4,8,4096]{2,1,0:T(8,128)S(1)} %copy-done, f32[2,8,4096]{2,1,0:T(8,128)S(1)} %get-tuple-element.41, f32[2,8,4096]{2,1,0:T(8,128)S(1)} %get-tuple-element.40, f32[2,8,4096]{2,1,0:T(8,128)S(1)} %get-tuple-element.45, f32[2,8,4096]{2,1,0:T(8,128)S(1)} %get-tuple-element.44, ...), kind=kLoop, calls=%fused_computation.38 | loop fusion | flops 1441792 | bytes 3145728 | tf_op jit(solution)/shard_map/add | solution.py:172
  52.8 24.1 %all-gather.2.cloned.1.call-done = f32[16,5,4096]{2,1,0:T(8,128)} async-done(((f32[1,5,4096]{2,1,0:T(8,128)}), f32[16,5,4096]{2,1,0:T(8,128)}) %all-gather.2.cloned.1.call-update) | async-done | bytes 1310736 | tf_op jit(solution)/shard_map/all_gather | solution.py:183
  76.9 1.7 %reduce_sum.32 = f32[5,4096]{1,0:T(8,128)S(1)} reduce(f32[16,5,4096]{2,1,0:T(8,128)} %all-gather.2.cloned.1.call-done, f32[]{:T(128)} %constant.14.clone.1), dimensions={0}, to_apply=%region_2.3 | reduce | flops 307200 | bytes 1392644 | tf_op jit(solution)/shard_map/reduce_sum | solution.py:184
  78.8 0.7 fusion.18
  (80 shorter events, 2.7 us)
Async XLA Ops:
  7.2 8.0 %copy-start = (f32[4,8,4096]{2,1,0:T(8,128)S(1)}, f32[4,8,4096]{2,1,0:T(8,128)}, u32[]{:S(2)}) copy-start(f32[4,8,4096]{2,1,0:T(8,128)} %param.11) | copy-start | bytes 1572868
  7.2 7.8 %copy-start.6 = (s32[4096]{0:T(1024)S(1)}, s32[4096]{0:T(1024)}, u32[]{:S(2)}) copy-start(s32[4096]{0:T(1024)} %param.15) | copy-start | bytes 49156
  7.2 7.9 %copy-start.1 = (f32[3,4096]{1,0:T(4,128)S(1)}, f32[3,4096]{1,0:T(4,128)}, u32[]{:S(2)}) copy-start(f32[3,4096]{1,0:T(4,128)} %param.14) | copy-start | bytes 147460
  7.2 69.7 %all-gather.2.cloned.1.call-start = ((), (), s32[]{:S(2)}) async-start(), calls=%async_computation | async-start | bytes 2228224 | tf_op jit(solution)/shard_map/all_gather | solution.py:183
  9.2 6.2 %copy-start.13 = (f32[8]{0:T(128)S(1)}, f32[8]{0:T(128)}, u32[]{:S(2)}) copy-start(f32[8]{0:T(128)} %param.19) | copy-start | bytes 100
  9.2 6.2 %copy-start.14 = (s32[8]{0:T(128)S(1)}, s32[8]{0:T(128)}, u32[]{:S(2)}) copy-start(s32[8]{0:T(128)} %param.18) | copy-start | bytes 100
  9.2 6.5 %copy-start.10 = (s32[8]{0:T(128)S(1)}, s32[8]{0:T(128)}, u32[]{:S(2)}) copy-start(s32[8]{0:T(128)} %param.20) | copy-start | bytes 100
  9.3 6.5 %copy-start.9 = (f32[4,8]{1,0:T(4,128)S(1)}, f32[4,8]{1,0:T(4,128)}, u32[]{:S(2)}) copy-start(f32[4,8]{1,0:T(4,128)} %param.17) | copy-start | bytes 388
  9.3 8.3 %collective-permute-start = (f32[4,8,1]{2,1,0:T(8,128)S(1)}, f32[4,8,1]{2,1,0:T(8,128)S(1)}, u32[]{:S(2)}, u32[]{:S(2)}) collective-permute-start(f32[4,8,1]{2,1,0:T(8,128)S(1)} %get-tuple-element.55), channel_id=1, source_target_pairs={{0,1},{1,2},{2,3},{3,4},{4,5},{5,6},{6,7},{7,8},{8,9},{9,10},{10,1... | collective-permute-start | bytes 392 | tf_op jit(solution)/shard_map/ppermute | solution.py:20
  13.7 4.7 %collective-permute-start.1 = (f32[4,8,1]{2,1,0:T(8,128)S(1)}, f32[4,8,1]{2,1,0:T(8,128)S(1)}, u32[]{:S(2)}, u32[]{:S(2)}) collective-permute-start(f32[4,8,1]{2,1,0:T(8,128)S(1)} %get-tuple-element.54), channel_id=1, source_target_pairs={{1,0},{2,1},{3,2},{4,3},{5,4},{6,5},{7,6},{8,7},{9,8},{10,9},{11,1... | collective-permute-start | bytes 392 | tf_op jit(solution)/shard_map/ppermute | solution.py:22
  18.7 0.7 copy-start.3
  19.7 6.4 %copy-start.12 = (f32[8]{0:T(128)S(1)}, f32[8]{0:T(128)}, u32[]{:S(2)}) copy-start(f32[8]{0:T(128)} %param.16) | copy-start | bytes 100
  19.8 6.6 %copy-start.11 = (f32[5]{0:T(128)S(1)}, f32[5]{0:T(128)}, u32[]{:S(2)}) copy-start(f32[5]{0:T(128)} %constant.9.clone) | copy-start | bytes 64
  20.6 6.5 %collective-permute-start.2 = (f32[4,8,1]{2,1,0:T(8,128)}, f32[4,8,1]{2,1,0:T(8,128)}, u32[]{:S(2)}, u32[]{:S(2)}) collective-permute-start(f32[4,8,1]{2,1,0:T(8,128)} %get-tuple-element.50), channel_id=1, source_target_pairs={{0,1},{1,2},{2,3},{3,4},{4,5},{5,6},{6,7},{7,8},{8,9},{9,10},{10,1... | collective-permute-start | bytes 392 | tf_op jit(solution)/shard_map/ppermute | solution.py:20
  24.7 5.6 %collective-permute-start.3 = (f32[4,8,1]{2,1,0:T(8,128)}, f32[4,8,1]{2,1,0:T(8,128)}, u32[]{:S(2)}, u32[]{:S(2)}) collective-permute-start(f32[4,8,1]{2,1,0:T(8,128)} %get-tuple-element.51), channel_id=1, source_target_pairs={{1,0},{2,1},{3,2},{4,3},{5,4},{6,5},{7,6},{8,7},{9,8},{10,9},{11,1... | collective-permute-start | bytes 392 | tf_op jit(solution)/shard_map/ppermute | solution.py:22
  26.4 5.2 %copy-start.4 = (f32[4096]{0:T(1024)S(1)}, f32[4096]{0:T(1024)}, u32[]{:S(2)}) copy-start(f32[4096]{0:T(1024)} %param.12) | copy-start | bytes 49156
  26.4 5.2 %copy-start.7 = (f32[4,8]{1,0:T(4,128)S(1)}, f32[4,8]{1,0:T(4,128)}, u32[]{:S(2)}) copy-start(f32[4,8]{1,0:T(4,128)} %get-tuple-element.85) | copy-start | bytes 388
  32.0 6.0 %collective-permute-start.4 = (f32[4,8,1]{2,1,0:T(8,128)S(1)}, f32[4,8,1]{2,1,0:T(8,128)S(1)}, u32[]{:S(2)}, u32[]{:S(2)}) collective-permute-start(f32[4,8,1]{2,1,0:T(8,128)S(1)} %get-tuple-element.46), channel_id=1, source_target_pairs={{0,1},{1,2},{2,3},{3,4},{4,5},{5,6},{6,7},{7,8},{8,9},{9,10},{10,1... | collective-permute-start | bytes 392 | tf_op jit(solution)/shard_map/ppermute | solution.py:20
  36.6 4.5 %collective-permute-start.5 = (f32[4,8,1]{2,1,0:T(8,128)S(1)}, f32[4,8,1]{2,1,0:T(8,128)S(1)}, u32[]{:S(2)}, u32[]{:S(2)}) collective-permute-start(f32[4,8,1]{2,1,0:T(8,128)S(1)} %get-tuple-element.47), channel_id=1, source_target_pairs={{1,0},{2,1},{3,2},{4,3},{5,4},{6,5},{7,6},{8,7},{9,8},{10,9},{11,1... | collective-permute-start | bytes 392 | tf_op jit(solution)/shard_map/ppermute | solution.py:22
  42.0 6.0 %collective-permute-start.6 = (f32[4,8,1]{2,1,0:T(8,128)S(1)}, f32[4,8,1]{2,1,0:T(8,128)S(1)}, u32[]{:S(2)}, u32[]{:S(2)}) collective-permute-start(f32[4,8,1]{2,1,0:T(8,128)S(1)} %get-tuple-element.42), channel_id=1, source_target_pairs={{0,1},{1,2},{2,3},{3,4},{4,5},{5,6},{6,7},{7,8},{8,9},{9,10},{10,1... | collective-permute-start | bytes 392 | tf_op jit(solution)/shard_map/ppermute | solution.py:20
  46.6 5.0 %copy-start.8 = (f32[4,8]{1,0:T(4,128)S(1)}, f32[4,8]{1,0:T(4,128)}, u32[]{:S(2)}) copy-start(f32[4,8]{1,0:T(4,128)} %pad_maximum_fusion.22) | copy-start | bytes 388
  46.6 4.5 %collective-permute-start.7 = (f32[4,8,1]{2,1,0:T(8,128)S(1)}, f32[4,8,1]{2,1,0:T(8,128)S(1)}, u32[]{:S(2)}, u32[]{:S(2)}) collective-permute-start(f32[4,8,1]{2,1,0:T(8,128)S(1)} %get-tuple-element.43), channel_id=1, source_target_pairs={{1,0},{2,1},{3,2},{4,3},{5,4},{6,5},{7,6},{8,7},{9,8},{10,9},{11,1... | collective-permute-start | bytes 392 | tf_op jit(solution)/shard_map/ppermute | solution.py:22
  51.8 27.0 %copy-start.5 = (f32[4096]{0:T(1024)S(1)}, f32[4096]{0:T(1024)}, u32[]{:S(2)}) copy-start(f32[4096]{0:T(1024)} %convert_element_type.10) | copy-start | bytes 49156
  78.6 0.8 copy-start.2
Sparse Core Ops, SparseCore 0:
  27.3 49.5 all-gather.1
